TPU v7x, 32 devices: a whole 2x2x4 slice. The times are simulated.
32 devices in a mesh: blk: 16 (over z, x, core), rep: 2 (over y).
Axes of the slice: x: 2, y: 2, z: 4, core: 2. Of those that a mesh axis runs over, the one named last changes fastest.
Arguments:
- users: float32 [32768, 256], P(('blk', 'rep')), may hold values from -1 to 1
- items: bfloat16 [32768, 256], P(('blk', 'rep')), may hold values from -1 to 1
- hot_factors: float32 [512, 256], P('rep'), may hold values from -1 to 1
- slot_items: int32 [4, 16, 32768], P(None, None, ('blk', 'rep')), may hold values from 0 to 1023
- slot_values: bfloat16 [4, 16, 32768], P(None, None, ('blk', 'rep')), may hold values from -5 to 5
- slot_lengths: int32 [4, 32768], P(None, ('blk', 'rep')), may hold values from 1 to 16
- hot_ids: int32 [8192], P(('blk', 'rep')), may hold values from 0 to 511
- hot_count: int32 [32], P(('blk', 'rep')), may hold values from 128 to 256
- hot_values: bfloat16 [32768, 256], P(('blk', 'rep')), may hold values from -5 to 5
- hot_lengths: int32 [32768], P(('blk', 'rep')), may hold values from 0 to 256
Outputs:
- new_users: float32 [32768, 256], P(('blk', 'rep'))
- new_items: bfloat16 [32768, 256], P(('blk', 'rep'))
- new_hot: float32 [512, 256], P('rep')
Inputs may be any that keep to these rules, and one draw needn't show every extreme that they name: `hot_ids`: ids may repeat within a device.
All inputs are finite; a program needn't handle non-finite values.
Results may differ from a plain program's by a relative error of at most 0.0015.
The roundings to bfloat16 on the way count: a program that leaves them out, or rounds other values in their place, can miss the bound.
Values may be sent and summed in bfloat16 or wider, within the bound.
A program may use at most 64 MiB of HBM per device.

v0:
```python
import jax
import jax.numpy as jnp
from jax import lax
from jax.sharding import PartitionSpec as P

LEARN_RATE = 0.03
DECAY_RATE = 0.02
LEARN_HOT = 0.005
HOT_USER_SCALE = 1.6


def from_behind(block, axis, distance):
    devices = range(lax.axis_size(axis))
    route = [((i - distance) % len(devices), i) for i in devices]
    return lax.ppermute(block, axis, route)


def build_block(slot_items, slot_values, slot_lengths, width):
    columns = lax.broadcasted_iota(jnp.int32, (slot_items.shape[1], width), 1)
    rating_sum = jnp.zeros((slot_items.shape[1], width), jnp.float32)
    rating_count = jnp.zeros((slot_items.shape[1], width), jnp.float32)
    for position in range(slot_items.shape[0]):
        slot_hit = (slot_items[position][:, None] == columns) & (position < slot_lengths)[:, None]
        rating_sum = rating_sum + jnp.where(
            slot_hit, slot_values[position].astype(jnp.float32)[:, None], jnp.float32(0.0)
        )
        rating_count = rating_count + slot_hit.astype(jnp.float32)
    return (rating_sum, rating_count)


def stop_update(user_rows, block, slot_items, slot_values, slot_lengths):
    user_bf = user_rows.astype(jnp.bfloat16)
    predicted = jnp.dot(user_bf, block.T, preferred_element_type=jnp.float32)
    rating_sum, rating_count = build_block(slot_items, slot_values, slot_lengths, block.shape[0])
    err_bf = (rating_sum - rating_count * predicted).astype(jnp.bfloat16)
    grad_users = jnp.dot(err_bf, block, preferred_element_type=jnp.float32)
    grad_items = jnp.dot(err_bf.T, user_bf, preferred_element_type=jnp.float32)
    block_float = block.astype(jnp.float32)
    new_rows = user_rows + LEARN_RATE * (grad_users - DECAY_RATE * user_rows)
    new_block = (block_float + LEARN_RATE * (grad_items - DECAY_RATE * block_float)).astype(
        jnp.bfloat16
    )
    return (new_rows, new_block)


def hot_terms(user_rows, hot_full, slot_ids, live_count, hot_values, hot_lengths):
    selector = (
        slot_ids[:, None]
        == lax.broadcasted_iota(jnp.int32, (slot_ids.shape[0], hot_full.shape[0]), 1)
    ).astype(jnp.float32)
    hot_slot_bf = jnp.dot(selector, hot_full, precision=lax.Precision.HIGHEST).astype(jnp.bfloat16)
    user_bf = user_rows.astype(jnp.bfloat16)
    hot_predicted = jnp.dot(user_bf, hot_slot_bf.T, preferred_element_type=jnp.float32)
    positions = lax.broadcasted_iota(jnp.int32, hot_values.shape, 1)
    valid = positions < jnp.minimum(hot_lengths, live_count[0])[:, None]
    hot_err_bf = jnp.where(
        valid, hot_values.astype(jnp.float32) - hot_predicted, jnp.float32(0.0)
    ).astype(jnp.bfloat16)
    slot_grads = jnp.dot(hot_err_bf.T, user_bf, preferred_element_type=jnp.float32)
    grad_dense = jnp.dot(selector.T, slot_grads, precision=lax.Precision.HIGHEST)
    pulled = jnp.dot(hot_err_bf, hot_slot_bf, preferred_element_type=jnp.float32)
    user_rate = HOT_USER_SCALE / hot_values.shape[1]
    new_rows = user_rows + user_rate * (pulled - DECAY_RATE * user_rows)
    return (new_rows, grad_dense)


def body(
    users,
    items,
    hot_factors,
    slot_items,
    slot_values,
    slot_lengths,
    hot_ids,
    hot_count,
    hot_values,
    hot_lengths,
):
    hot_full = lax.all_gather(hot_factors.astype(jnp.bfloat16), "rep", axis=0, tiled=True).astype(
        hot_factors.dtype
    )
    users, grad_dense = hot_terms(users, hot_full, hot_ids, hot_count, hot_values, hot_lengths)
    rows_owned = hot_factors.shape[0]
    grad_sum = lax.psum(grad_dense, ("blk", "rep"))
    own_rows = lax.dynamic_slice_in_dim(grad_sum, lax.axis_index("rep") * rows_owned, rows_owned, 0)
    new_hot = hot_factors + LEARN_HOT * (own_rows - DECAY_RATE * hot_factors)
    for stop_index in range(slot_items.shape[0]):
        users, items = stop_update(
            users, items, slot_items[stop_index], slot_values[stop_index], slot_lengths[stop_index]
        )
        items = from_behind(items, ("blk", "rep"), 1)
    return (users, items, new_hot)


def solution(mesh):
    return jax.shard_map(
        body,
        mesh=mesh,
        in_specs=(
            P(("blk", "rep"), None),
            P(("blk", "rep"), None),
            P("rep", None),
            P(None, None, ("blk", "rep")),
            P(None, None, ("blk", "rep")),
            P(None, ("blk", "rep")),
            P(("blk", "rep")),
            P(("blk", "rep")),
            P(("blk", "rep"), None),
            P(("blk", "rep")),
        ),
        out_specs=(P(("blk", "rep"), None), P(("blk", "rep"), None), P("rep", None)),
        check_vma=False,
    )
```

profile of v0, /device:TPU:1, one launch (start us, length us, event | category | flops | bytes accessed | tf_op | source)
XLA Modules:
  0.0 268.6 jit_solution(16747290715959294058)
XLA Ops:
  7.2 0.0 all-reduce.2.cloned.1.call-start
  7.2 1.0 fusion.115
  8.3 1.4 fusion.114
  9.7 1.0 slice_convert_fusion.63
  10.7 1.3 slice_convert_fusion
  12.6 2.4 compare_reduce_fusion.13
  15.1 1.0 convert_element_type.898
  16.0 5.9 %all_gather.3 = bf16[512,256]{1,0:T(8,128)(2,1)S(1)} all-gather(bf16[256,256]{1,0:T(8,128)(2,1)S(1)} %convert_element_type.898), channel_id=1, replica_groups=mesh['blk'=16,'rep'=2] {'rep'}, dimensions={0}, use_global_device_ids=true | all-gather | bytes 393216 | tf_op jit(solution)/shard_map/all_gather | solution.py:79
  22.0 1.2 copy.13
  23.3 0.3 convolution_convert_fusion
  23.5 0.0 copy-done
  23.6 0.0 copy-start.5
  23.6 0.4 fusion.78
  23.9 0.4 fusion.65
  24.3 0.3 copy-done.5
  24.6 23.2 %subtract_convert_fusion.3 = bf16[1024,1024]{1,0:T(8,128)(2,1)S(1)} fusion(bf16[1024,256]{1,0:T(8,128)(2,1)S(1)} %copy-done.5, f32[1024]{0:T(1024)S(1)} %bitcast.261, s32[1024]{0:T(1024)S(1)} %bitcast.241, f32[1024]{0:T(1024)S(1)} %bitcast.262, s32[1024]{0:T(1024)S(1)} %bitcast.242, f32[1024]{0:T(1024)S(1)} %bitcast.263, s32[1024]{0:T(1024)S(1)} %bitcast.243, ...), kind=kOutput, calls=%fused_computation.51 | convolution fusion | flops 638844928 | bytes 3817472 | tf_op jit(solution)/shard_map/dot_general | solution.py:33
  47.8 0.0 copy-start.6
  47.9 0.8 fusion.79
  48.6 0.0 copy-start.4
  48.7 1.2 collective-permute-start
  49.9 0.1 fusion.112
  49.9 0.1 fusion.113
  50.0 0.3 fusion.107
  50.3 0.1 slice_convert_fusion.1
  50.4 0.7 fusion.77
  51.1 12.7 %collective-permute-done = bf16[1024,256]{1,0:T(8,128)(2,1)S(1)} collective-permute-done((bf16[1024,256]{1,0:T(8,128)(2,1)S(1)}, bf16[1024,256]{1,0:T(8,128)(2,1)S(1)}, u32[]{:S(2)}, u32[]{:S(2)}) %collective-permute-start) | collective-permute-done | bytes 524320 | tf_op jit(solution)/shard_map/ppermute | solution.py:15
  63.8 23.2 %subtract_convert_fusion.2 = bf16[1024,1024]{1,0:T(8,128)(2,1)S(1)} fusion(bf16[1024,256]{1,0:T(8,128)(2,1)S(1)} %collective-permute-done, f32[1024]{0:T(1024)S(1)} %bitcast.282, s32[1024]{0:T(1024)S(1)} %bitcast.270, f32[1024]{0:T(1024)S(1)} %bitcast.283, s32[1024]{0:T(1024)S(1)} %bitcast.271, f32[1024]{0:T(1024)S(1)} %bitcast.284, ...), kind=kOutput, calls=%fused_computation.34 | convolution fusion | flops 638844928 | bytes 3817472 | tf_op jit(solution)/shard_map/dot_general | solution.py:33
  87.0 0.8 fusion.82
  87.8 0.1 collective-permute-start.1
  87.9 0.1 slice_convert_fusion.15
  87.9 0.7 fusion.73
  88.7 13.4 %collective-permute-done.1 = bf16[1024,256]{1,0:T(8,128)(2,1)S(1)} collective-permute-done((bf16[1024,256]{1,0:T(8,128)(2,1)S(1)}, bf16[1024,256]{1,0:T(8,128)(2,1)S(1)}, u32[]{:S(2)}, u32[]{:S(2)}) %collective-permute-start.1) | collective-permute-done | bytes 524320 | tf_op jit(solution)/shard_map/ppermute | solution.py:15
  102.1 23.4 %subtract_convert_fusion.1 = bf16[1024,1024]{1,0:T(8,128)(2,1)S(1)} fusion(bf16[1024,256]{1,0:T(8,128)(2,1)S(1)} %collective-permute-done.1, f32[1024]{0:T(1024)S(1)} %bitcast.277, s32[1024]{0:T(1024)S(1)} %bitcast.211, f32[1024]{0:T(1024)S(1)} %bitcast.278, s32[1024]{0:T(1024)S(1)} %bitcast.212, f32[1024]{0:T(1024)S(1)} %bitcast.279, ...), kind=kOutput, calls=%fused_computation.17 | convolution fusion | flops 638844928 | bytes 3817472 | tf_op jit(solution)/shard_map/dot_general | solution.py:33
  125.5 1.6 fusion.85
  127.1 0.0 collective-permute-start.2
  127.1 1.5 fusion.89
  128.6 0.0 all-reduce.2.cloned.1.call-update
  128.6 0.0 copy-start.9
  128.7 2.3 fusion.71
  131.0 11.2 %collective-permute-done.2 = bf16[1024,256]{1,0:T(8,128)(2,1)S(1)} collective-permute-done((bf16[1024,256]{1,0:T(8,128)(2,1)}, bf16[1024,256]{1,0:T(8,128)(2,1)S(1)}, u32[]{:S(2)}, u32[]{:S(2)}) %collective-permute-start.2) | collective-permute-done | bytes 524320 | tf_op jit(solution)/shard_map/ppermute | solution.py:15
  142.3 23.6 %subtract_convert_fusion = bf16[1024,1024]{1,0:T(8,128)(2,1)S(1)} fusion(bf16[1024,256]{1,0:T(8,128)(2,1)S(1)} %collective-permute-done.2, f32[1024]{0:T(1024)S(1)} %bitcast.176, s32[1024]{0:T(1024)S(1)} %bitcast.175, f32[1024]{0:T(1024)S(1)} %bitcast.210, s32[1024]{0:T(1024)S(1)} %bitcast.200, f32[1024]{0:T(1024)S(1)} %bitcast.217, s32[1024]{0:T(1024)S(1)} %bitcast.178, ...), kind=kOutput, calls=%fused_computation | convolution fusion | flops 638844928 | bytes 3817472 | tf_op jit(solution)/shard_map/dot_general | solution.py:33
  165.9 0.0 copy-start.3
  165.9 0.8 fusion.88
  166.7 0.5 copy-done.2
  167.3 88.7 %all-reduce.2.cloned.1.call-done = f32[512,256]{1,0:T(8,128)} async-done(((f32[512,256]{1,0:T(8,128)}), f32[512,256]{1,0:T(8,128)}) %all-reduce.2.cloned.1.call-update) | async-done | bytes 524304 | tf_op jit(solution)/shard_map/psum | solution.py:84
  256.0 1.7 multiply_add_fusion
  257.7 3.3 %fusion.69 = f32[1024,256]{1,0:T(8,128)} fusion(f32[1024,256]{1,0:T(8,128)S(1)} %fusion.71, bf16[1024,1024]{1,0:T(8,128)(2,1)} %copy-done.2, bf16[1024,256]{1,0:T(8,128)(2,1)S(1)} %collective-permute-done.2), kind=kOutput, calls=%fused_computation.140 | convolution fusion | flops 537919488 | bytes 4718592 | tf_op jit(solution)/shard_map/dot_general | solution.py:36
  261.0 0.8 copy.17
  (37 shorter events, 0.1 us)
Async XLA Ops:
  7.2 16.1 %copy-start.7 = (s32[1024]{0:T(1024)S(1)}, s32[1024]{0:T(1024)}, u32[]{:S(2)}) copy-start(s32[1024]{0:T(1024)} %param.19) | copy-start | bytes 12292
  7.2 16.1 %copy-start.8 = (s32[256]{0:T(256)S(1)}, s32[256]{0:T(256)}, u32[]{:S(2)}) copy-start(s32[256]{0:T(256)} %param.16) | copy-start | bytes 3076
  7.2 16.4 %copy-start = (f32[1024,256]{1,0:T(8,128)S(1)}, f32[1024,256]{1,0:T(8,128)}, u32[]{:S(2)}) copy-start(f32[1024,256]{1,0:T(8,128)} %param.10) | copy-start | bytes 3145732
  7.2 248.8 %all-reduce.2.cloned.1.call-start = ((), (), s32[]{:S(2)}) async-start(), calls=%async_computation | async-start | bytes 1048576 | tf_op jit(solution)/shard_map/psum | solution.py:84
  23.6 1.0 copy-start.5
  47.8 2.0 copy-start.6
  48.6 1.7 copy-start.4
  48.7 15.1 %collective-permute-start = (bf16[1024,256]{1,0:T(8,128)(2,1)S(1)}, bf16[1024,256]{1,0:T(8,128)(2,1)S(1)}, u32[]{:S(2)}, u32[]{:S(2)}) collective-permute-start(bf16[1024,256]{1,0:T(8,128)(2,1)S(1)} %fusion.79), channel_id=1, source_target_pairs={{31,0},{0,1},{1,2},{2,3},{3,4},{4,5},{5,6},{6,7},{7,8},{8,9},{9,10... | collective-permute-start | bytes 1572872 | tf_op jit(solution)/shard_map/ppermute | solution.py:15
  87.8 14.3 %collective-permute-start.1 = (bf16[1024,256]{1,0:T(8,128)(2,1)S(1)}, bf16[1024,256]{1,0:T(8,128)(2,1)S(1)}, u32[]{:S(2)}, u32[]{:S(2)}) collective-permute-start(bf16[1024,256]{1,0:T(8,128)(2,1)S(1)} %fusion.82), channel_id=1, source_target_pairs={{31,0},{0,1},{1,2},{2,3},{3,4},{4,5},{5,6},{6,7},{7,8},{8,9},{9,10... | collective-permute-start | bytes 1572872 | tf_op jit(solution)/shard_map/ppermute | solution.py:15
  125.5 1.6 copy-start.1
  127.1 15.1 %collective-permute-start.2 = (bf16[1024,256]{1,0:T(8,128)(2,1)}, bf16[1024,256]{1,0:T(8,128)(2,1)S(1)}, u32[]{:S(2)}, u32[]{:S(2)}) collective-permute-start(bf16[1024,256]{1,0:T(8,128)(2,1)} %fusion.85), channel_id=1, source_target_pairs={{31,0},{0,1},{1,2},{2,3},{3,4},{4,5},{5,6},{6,7},{7,8},{8,9},{9,10... | collective-permute-start | bytes 1572872 | tf_op jit(solution)/shard_map/ppermute | solution.py:15
  128.6 13.6 %copy-start.9 = (pred[1024]{0:T(1024)(128)(4,1)S(1)}, pred[1024]{0:T(1024)(128)(4,1)}, u32[]{:S(2)}) copy-start(pred[1024]{0:T(1024)(128)(4,1)} %get-tuple-element.54) | copy-start | bytes 3076
  128.6 13.6 %copy-start.10 = (pred[1024]{0:T(1024)(128)(4,1)S(1)}, pred[1024]{0:T(1024)(128)(4,1)}, u32[]{:S(2)}) copy-start(pred[1024]{0:T(1024)(128)(4,1)} %get-tuple-element.55) | copy-start | bytes 3076
  128.6 13.6 %copy-start.11 = (pred[1024]{0:T(1024)(128)(4,1)S(1)}, pred[1024]{0:T(1024)(128)(4,1)}, u32[]{:S(2)}) copy-start(pred[1024]{0:T(1024)(128)(4,1)} %get-tuple-element.56) | copy-start | bytes 3076
  128.6 13.6 %copy-start.12 = (pred[1024]{0:T(1024)(128)(4,1)S(1)}, pred[1024]{0:T(1024)(128)(4,1)}, u32[]{:S(2)}) copy-start(pred[1024]{0:T(1024)(128)(4,1)} %get-tuple-element.57) | copy-start | bytes 3076
  128.6 13.6 %copy-start.13 = (pred[1024]{0:T(1024)(128)(4,1)S(1)}, pred[1024]{0:T(1024)(128)(4,1)}, u32[]{:S(2)}) copy-start(pred[1024]{0:T(1024)(128)(4,1)} %get-tuple-element.58) | copy-start | bytes 3076
  128.7 13.6 %copy-start.14 = (pred[1024]{0:T(1024)(128)(4,1)S(1)}, pred[1024]{0:T(1024)(128)(4,1)}, u32[]{:S(2)}) copy-start(pred[1024]{0:T(1024)(128)(4,1)} %get-tuple-element.59) | copy-start | bytes 3076
  128.7 13.6 %copy-start.15 = (pred[1024]{0:T(1024)(128)(4,1)S(1)}, pred[1024]{0:T(1024)(128)(4,1)}, u32[]{:S(2)}) copy-start(pred[1024]{0:T(1024)(128)(4,1)} %get-tuple-element.213) | copy-start | bytes 3076
  128.7 13.6 %copy-start.16 = (pred[1024]{0:T(1024)(128)(4,1)S(1)}, pred[1024]{0:T(1024)(128)(4,1)}, u32[]{:S(2)}) copy-start(pred[1024]{0:T(1024)(128)(4,1)} %get-tuple-element.232) | copy-start | bytes 3076
  128.7 13.6 %copy-start.17 = (pred[1024]{0:T(1024)(128)(4,1)S(1)}, pred[1024]{0:T(1024)(128)(4,1)}, u32[]{:S(2)}) copy-start(pred[1024]{0:T(1024)(128)(4,1)} %get-tuple-element.236) | copy-start | bytes 3076
  128.7 13.6 %copy-start.18 = (pred[1024]{0:T(1024)(128)(4,1)S(1)}, pred[1024]{0:T(1024)(128)(4,1)}, u32[]{:S(2)}) copy-start(pred[1024]{0:T(1024)(128)(4,1)} %get-tuple-element.237) | copy-start | bytes 3076
  128.7 13.6 %copy-start.19 = (pred[1024]{0:T(1024)(128)(4,1)S(1)}, pred[1024]{0:T(1024)(128)(4,1)}, u32[]{:S(2)}) copy-start(pred[1024]{0:T(1024)(128)(4,1)} %get-tuple-element.238) | copy-start | bytes 3076
  128.7 13.6 %copy-start.20 = (pred[1024]{0:T(1024)(128)(4,1)S(1)}, pred[1024]{0:T(1024)(128)(4,1)}, u32[]{:S(2)}) copy-start(pred[1024]{0:T(1024)(128)(4,1)} %get-tuple-element.239) | copy-start | bytes 3076
  165.9 1.4 copy-start.2
  165.9 90.1 %copy-start.3 = (f32[256,256]{1,0:T(8,128)S(1)}, f32[256,256]{1,0:T(8,128)}, u32[]{:S(2)}) copy-start(f32[256,256]{1,0:T(8,128)} %param.12) | copy-start | bytes 786436
  167.3 93.7 %collective-permute-start.3 = (bf16[1024,256]{1,0:T(8,128)(2,1)S(1)}, bf16[1024,256]{1,0:T(8,128)(2,1)S(1)}, u32[]{:S(2)}, u32[]{:S(2)}) collective-permute-start(bf16[1024,256]{1,0:T(8,128)(2,1)S(1)} %fusion.88), channel_id=1, source_target_pairs={{31,0},{0,1},{1,2},{2,3},{3,4},{4,5},{5,6},{6,7},{7,8},{8,9},{9,10... | collective-permute-start | bytes 1572872 | tf_op jit(solution)/shard_map/ppermute | solution.py:15
Sparse Core Ops, SparseCore 0:
  128.7 127.2 all-reduce.1
where the time goes:
time: 271 us; the launch traced here: 269 us
  waiting for transfers between devices  126 us (46%)
  matrix products  107 us (39%)
  between operations  15.1 us (6%)
  other arithmetic  7.52 us (3%)
  blocking collectives  5.95 us (2%)
  local copies, waits for them, and re-layouts  5.48 us (2%)
    dot_general x4, matrix products, stop_update(): predicted = jnp.dot(user_bf, block.T, preferred_element_type=jnp.float32)  93.4 us
    psum x1, waiting for transfers between devices, body(): grad_sum = lax.psum(grad_dense, ('blk', 'rep'))  88.7 us
    ppermute x4, waiting for transfers between devices, from_behind(): return lax.ppermute(block, axis, route)  37.3 us
    dot_general x4, matrix products, stop_update(): grad_users = jnp.dot(err_bf, block, preferred_element_type=jnp.float32)  7.02 us
    all_gather x1, blocking collectives, body(): lax.all_gather(hot_factors.astype(jnp.bfloat16), 'rep', axis=0, tiled=True)  5.95 us
  transfers between devices with their start and end apart: 5, of which 4 were waited for; matrix products, arithmetic and copies ran while one was open for 13% of the time, Pallas kernels for 0%

commit v1 on v0

v1 whole, which is shorter than its diff:
```python
import functools

import jax
import jax.numpy as jnp
from jax import lax
from jax.experimental import pallas as pl
from jax.experimental.pallas import tpu as pltpu
from jax.sharding import PartitionSpec as P

LEARN_RATE = 0.03
DECAY_RATE = 0.02
LEARN_HOT = 0.005
HOT_USER_SCALE = 1.6

F32 = jnp.float32
BF16 = jnp.bfloat16
MESH = pl.DeviceIdType.MESH
GROUP = 16
LO = 128
CHUNK = 256


def nn(a, b):
    return lax.dot_general(a, b, (((1,), (0,)), ((), ())), preferred_element_type=F32)


def nt(a, b):
    return lax.dot_general(a, b, (((1,), (1,)), ((), ())), preferred_element_type=F32)


def iota(shape, dim):
    return lax.broadcasted_iota(jnp.int32, shape, dim)


def one_hot(mask):
    return jnp.where(mask, 1.0, 0.0).astype(F32)


def reduce_plan(n_blk, rows):
    plan, held, bit = [], rows, 1
    while bit < n_blk:
        halve = held >= 32
        plan.append((bit, held, halve))
        held = held // 2 if halve else held
        bit *= 2
    return plan, held


def kernel(
    n_blk,
    n_rep,
    users_ref,
    items_ref,
    hot_ref,
    slot_items_ref,
    slot_values_ref,
    slot_lengths_ref,
    hot_ids_ref,
    hot_count_ref,
    hot_values_ref,
    hot_lengths_ref,
    users_out,
    items_out,
    hot_out,
    eye,
    hot_full,
    codes,
    rating_sum,
    rating_count,
    err,
    user_bf,
    user_t,
    grad_users,
    blocks,
    sent,
    last,
    grads,
    reps_in,
    hot_new,
    *rest,
):
    users_n, rank = users_ref.shape
    stops, slots, _ = slot_items_ref.shape
    width = items_ref.shape[0]
    n_chunks = width // CHUNK
    own_hot = hot_ref.shape[0]
    hot_slots = hot_values_ref.shape[1]
    plan, held_rows = reduce_plan(n_blk, own_hot)
    red_in = rest[: len(plan)]
    (
        block_send,
        block_recv,
        gather_send,
        gather_recv,
        red_send,
        red_recv,
        rep_send,
        rep_recv,
        back_send,
        back_recv,
    ) = rest[len(plan) :]

    b, r = lax.axis_index("blk"), lax.axis_index("rep")
    wrap = r == n_rep - 1
    nxt = (jnp.where(wrap, lax.rem(b + 1, n_blk), b), lax.rem(r + 1, n_rep))
    first = r == 0
    prv = (jnp.where(first, lax.rem(b + n_blk - 1, n_blk), b), lax.rem(r + n_rep - 1, n_rep))

    def bit_of(bit):
        return lax.rem(b // bit, 2)

    def partner(bit):
        return (b + bit * (1 - 2 * bit_of(bit)), r)

    def rep_peer(k):
        return (b, lax.rem(r + k, n_rep))

    barrier = pltpu.get_barrier_semaphore()
    peers = [nxt, prv] + [partner(bit) for bit, _, _ in plan] + [rep_peer(k) for k in range(1, n_rep)]
    for peer in peers:
        pl.semaphore_signal(barrier, inc=1, device_id=peer, device_id_type=MESH)
    pl.semaphore_wait(barrier, len(peers))

    own_at = pl.ds(pl.multiple_of(r * own_hot, own_hot), own_hot)
    hot_full[own_at, :] = hot_ref[...].astype(BF16)
    gathers = []
    for k in range(1, n_rep):
        copy = pltpu.make_async_remote_copy(
            src_ref=hot_full.at[own_at],
            dst_ref=hot_full.at[own_at],
            send_sem=gather_send.at[k - 1],
            recv_sem=gather_recv.at[k - 1],
            device_id=rep_peer(k),
            device_id_type=MESH,
        )
        copy.start()
        gathers.append(copy)

    eye[...] = one_hot(iota(eye.shape, 0) == iota(eye.shape, 1)).astype(BF16)

    def to_blocks(c, carry):
        rows = items_ref[pl.ds(pl.multiple_of(c * CHUNK, CHUNK), CHUNK), :]
        blocks[0, c] = nt(eye[...], rows).astype(BF16)
        return carry

    lax.fori_loop(0, n_chunks, to_blocks, 0)

    lines = 3 * slots
    cols = slots * GROUP
    n_groups = users_n // GROUP

    def expand(t):
        item = slot_items_ref[t]
        live = iota(item.shape, 0) < slot_lengths_ref[pl.ds(t, 1), :]
        place = lax.rem(iota(item.shape, 1), GROUP)
        code = jnp.where(live, (item // LO) * GROUP + place, -1)
        low = lax.rem(item, LO)
        stacked = jnp.concatenate(
            [code.astype(F32).astype(BF16), low.astype(F32).astype(BF16), slot_values_ref[t]], axis=0
        )
        spread = one_hot(iota((lines * GROUP, lines), 0) // GROUP == iota((lines * GROUP, lines), 1))
        wide = nn(spread.astype(BF16), stacked)
        same = lax.rem(iota(wide.shape, 0), GROUP) == lax.rem(iota(wide.shape, 1), GROUP)
        wide = jnp.where(same, wide, 0.0).astype(BF16)
        member = one_hot(iota((n_groups, users_n), 1) // GROUP == iota((n_groups, users_n), 0))
        codes[...] = nt(member.astype(BF16), wide)

        def eight(i, carry):
            packed = codes[pl.ds(pl.multiple_of(i * 8, 8), 8), :]
            levels = iota((LO, cols), 0).astype(F32)
            for j in range(8):
                line = packed[j : j + 1, :]
                left = one_hot(levels == line[:, :cols]).astype(BF16)
                hit = levels == line[:, cols : 2 * cols]
                right = jnp.concatenate(
                    [
                        jnp.where(hit, line[:, 2 * cols :], 0.0).astype(BF16),
                        one_hot(hit).astype(BF16),
                    ],
                    axis=0,
                )
                both = nt(left, right)
                at = pl.ds(pl.multiple_of(i * 8 * GROUP + j * GROUP, GROUP), GROUP)
                for h in range(width // LO):
                    part = both[h * GROUP : (h + 1) * GROUP, :]
                    rating_sum[at, h * LO : (h + 1) * LO] = part[:, :LO]
                    rating_count[at, h * LO : (h + 1) * LO] = part[:, LO:].astype(BF16)
            return carry

        lax.fori_loop(0, n_groups // 8, eight, 0)

    def transpose_users():
        for i in range(users_n // CHUNK):
            rows = slice(i * CHUNK, (i + 1) * CHUNK)
            user_t[:, rows] = nt(eye[...], user_bf[rows, :]).astype(BF16)

    user_bf[...] = users_ref[...].astype(BF16)
    transpose_users()
    expand(0)

    for copy in gathers:
        copy.wait()
    hot_total = hot_full.shape[0]
    hot_t = jnp.concatenate(
        [
            nt(eye[...], hot_full[i * own_hot : (i + 1) * own_hot, :]).astype(BF16)
            for i in range(hot_total // own_hot)
        ],
        axis=1,
    )
    selector = one_hot(iota((hot_total, hot_slots), 0) == hot_ids_ref[...]).astype(BF16)
    hot_slot_t = nn(hot_t, selector).astype(BF16)
    limit = jnp.minimum(hot_lengths_ref[...], hot_count_ref[0]).astype(F32).astype(BF16)
    user_rate = HOT_USER_SCALE / hot_slots
    for i in range(users_n // CHUNK):
        rows = slice(i * CHUNK, (i + 1) * CHUNK)
        predicted = nn(user_bf[rows, :], hot_slot_t)
        bound = nt(eye[...], jnp.broadcast_to(limit[:, rows], (hot_slots, CHUNK)))
        valid = iota(predicted.shape, 1).astype(F32) < bound
        hot_err = jnp.where(valid, hot_values_ref[rows, :].astype(F32) - predicted, 0.0).astype(BF16)
        err[rows, :] = hot_err
        pulled = nt(hot_err, hot_slot_t)
        old = users_ref[rows, :]
        users_out[rows, :] = old + user_rate * (pulled - DECAY_RATE * old)
    slot_grads = nn(user_t[...], err[...])
    dense = jnp.zeros((hot_total, rank), F32)
    for _ in range(3):
        piece = slot_grads.astype(BF16)
        dense = dense + nt(selector, piece)
        slot_grads = slot_grads - piece.astype(F32)
    for i in range(n_rep):
        grads[i] = dense[i * own_hot : (i + 1) * own_hot, :]

    def reduce_steps():
        low = 0
        for i, (bit, held, halve) in enumerate(plan):
            n = held // 2 if halve else held
            away = low + n * (1 - bit_of(bit)) if halve else low
            low = low + n * bit_of(bit) if halve else low
            copy = pltpu.make_async_remote_copy(
                src_ref=grads.at[:, pl.ds(pl.multiple_of(away, 16), n), :],
                dst_ref=red_in[i],
                send_sem=red_send.at[i],
                recv_sem=red_recv.at[i],
                device_id=partner(bit),
                device_id_type=MESH,
            )
            copy.start()
            yield
            copy.wait()
            at = pl.ds(pl.multiple_of(low, 16), n)
            grads[:, at, :] = grads[:, at, :] + red_in[i][...]
        at = pl.ds(pl.multiple_of(low, 16), held_rows)
        copies = []
        for k in range(1, n_rep):
            copy = pltpu.make_async_remote_copy(
                src_ref=grads.at[lax.rem(r + k, n_rep), at, :],
                dst_ref=reps_in.at[k - 1],
                send_sem=rep_send.at[k - 1],
                recv_sem=rep_recv.at[k - 1],
                device_id=rep_peer(k),
                device_id_type=MESH,
            )
            copy.start()
            copies.append(copy)
        yield
        total = grads[r, at, :]
        for k, copy in enumerate(copies):
            copy.wait()
            total = total + reps_in[k]
        old = hot_ref[at, :]
        hot_new[at, :] = old + LEARN_HOT * (total - DECAY_RATE * old)
        for i, (bit, held, halve) in reversed(list(enumerate(plan))):
            if not halve:
                continue
            n = held // 2
            at = pl.ds(pl.multiple_of(low, 16), n)
            copy = pltpu.make_async_remote_copy(
                src_ref=hot_new.at[at],
                dst_ref=hot_new.at[at],
                send_sem=back_send.at[i],
                recv_sem=back_recv.at[i],
                device_id=partner(bit),
                device_id_type=MESH,
            )
            copy.start()
            yield
            copy.wait()
            low = low - n * bit_of(bit)

    steps = reduce_steps()

    def move(t, c):
        at = pl.ds(pl.multiple_of(c * CHUNK, CHUNK), CHUNK)
        return pltpu.make_async_remote_copy(
            src_ref=sent.at[t, c],
            dst_ref=last.at[at] if t == stops - 1 else blocks.at[t + 1, c],
            send_sem=block_send.at[t, c],
            recv_sem=block_recv.at[t, c],
            device_id=nxt,
            device_id_type=MESH,
        )

    def chunk(t, c, carry):
        if t > 0:
            move(t - 1, c).wait_recv()
        block = blocks[t, c]
        lanes = pl.ds(pl.multiple_of(c * CHUNK, CHUNK), CHUNK)
        for i in range(users_n // CHUNK):
            rows = slice(i * CHUNK, (i + 1) * CHUNK)
            predicted = nn(user_bf[rows, :], block)
            errors = rating_sum[rows, lanes] - rating_count[rows, lanes].astype(F32) * predicted
            errors = errors.astype(BF16)
            err[rows, :] = errors
            grad_users[rows, :] += nt(errors, block)
        grad_items = nn(user_t[...], err[...])
        held = block.astype(F32)
        new = (held + LEARN_RATE * (grad_items - DECAY_RATE * held)).astype(BF16)
        if t == stops - 1:
            new = nt(eye[...], new).astype(BF16)
        sent[t, c] = new
        move(t, c).start()
        return carry

    for t in range(stops):
        user_bf[...] = users_out[...].astype(BF16)
        transpose_users()
        grad_users[...] = jnp.zeros_like(grad_users)
        if t > 0:
            expand(t)
            next(steps, None)
        half = n_chunks // 2
        lax.fori_loop(0, half, functools.partial(chunk, t), 0)
        next(steps, None)
        lax.fori_loop(half, n_chunks, functools.partial(chunk, t), 0)
        next(steps, None)
        old = users_out[...]
        users_out[...] = old + LEARN_RATE * (grad_users[...] - DECAY_RATE * old)

    for _ in steps:
        pass
    hot_out[...] = hot_new[...]

    def finish(c, carry):
        move(stops - 1, c).wait_recv()
        at = pl.ds(pl.multiple_of(c * CHUNK, CHUNK), CHUNK)
        items_out[at, :] = last[at, :]
        return carry

    lax.fori_loop(0, n_chunks, finish, 0)
    for t in range(stops):

        def drain(c, carry, t=t):
            move(t, c).wait_send()
            return carry

        lax.fori_loop(0, n_chunks, drain, 0)


def body(
    n_blk,
    n_rep,
    users,
    items,
    hot_factors,
    slot_items,
    slot_values,
    slot_lengths,
    hot_ids,
    hot_count,
    hot_values,
    hot_lengths,
):
    users_n, rank = users.shape
    width = items.shape[0]
    stops, slots, _ = slot_items.shape
    own_hot = hot_factors.shape[0]
    n_chunks = width // CHUNK
    plan, held_rows = reduce_plan(n_blk, own_hot)
    dma = pltpu.SemaphoreType.DMA
    vmem = pl.BlockSpec(memory_space=pltpu.VMEM)
    specs = [vmem] * 10
    specs[7] = pl.BlockSpec(memory_space=pltpu.SMEM)
    scratch = [
        pltpu.VMEM((CHUNK, CHUNK), BF16),
        pltpu.VMEM((n_rep * own_hot, rank), BF16),
        pltpu.VMEM((users_n // GROUP, 3 * slots * GROUP), F32),
        pltpu.VMEM((users_n, width), F32),
        pltpu.VMEM((users_n, width), BF16),
        pltpu.VMEM((users_n, CHUNK), BF16),
        pltpu.VMEM((users_n, rank), BF16),
        pltpu.VMEM((rank, users_n), BF16),
        pltpu.VMEM((users_n, rank), F32),
        pltpu.VMEM((stops, n_chunks, rank, CHUNK), BF16),
        pltpu.VMEM((stops, n_chunks, rank, CHUNK), BF16),
        pltpu.VMEM((width, rank), BF16),
        pltpu.VMEM((n_rep, own_hot, rank), F32),
        pltpu.VMEM((max(n_rep - 1, 1), held_rows, rank), F32),
        pltpu.VMEM((own_hot, rank), F32),
    ]
    for _, held, halve in plan:
        scratch.append(pltpu.VMEM((n_rep, held // 2 if halve else held, rank), F32))
    bits = max(len(plan), 1)
    others = max(n_rep - 1, 1)
    scratch += [
        dma((stops, n_chunks)),
        dma((stops, n_chunks)),
        dma((others,)),
        dma((others,)),
        dma((bits,)),
        dma((bits,)),
        dma((others,)),
        dma((others,)),
        dma((bits,)),
        dma((bits,)),
    ]
    return tuple(
        pl.pallas_call(
            functools.partial(kernel, n_blk, n_rep),
            out_shape=(
                jax.ShapeDtypeStruct(users.shape, F32),
                jax.ShapeDtypeStruct(items.shape, BF16),
                jax.ShapeDtypeStruct(hot_factors.shape, F32),
            ),
            in_specs=specs,
            out_specs=(vmem, vmem, vmem),
            scratch_shapes=scratch,
            compiler_params=pltpu.CompilerParams(
                collective_id=0, has_side_effects=True, vmem_limit_bytes=48 * 2**20
            ),
        )(
            users,
            items,
            hot_factors,
            slot_items,
            slot_values,
            slot_lengths,
            hot_ids.reshape(1, -1),
            hot_count,
            hot_values,
            hot_lengths.reshape(1, -1),
        )
    )


def solution(mesh):
    return jax.shard_map(
        functools.partial(body, mesh.shape["blk"], mesh.shape["rep"]),
        mesh=mesh,
        in_specs=(
            P(("blk", "rep"), None),
            P(("blk", "rep"), None),
            P("rep", None),
            P(None, None, ("blk", "rep")),
            P(None, None, ("blk", "rep")),
            P(None, ("blk", "rep")),
            P(("blk", "rep")),
            P(("blk", "rep")),
            P(("blk", "rep"), None),
            P(("blk", "rep")),
        ),
        out_specs=(P(("blk", "rep"), None), P(("blk", "rep"), None), P("rep", None)),
        check_vma=False,
    )
```

time: 271 us -> 76.8 us (0.28)
  waiting for transfers between devices: 126 us -> 0 us
  matrix products: 107 us -> 0 us
  Pallas kernels: 0 us -> 65.1 us
  between operations: 15.1 us -> 1.33 us
  other arithmetic: 7.52 us -> 0 us
  blocking collectives: 5.95 us -> 0 us
  local copies, waits for them, and re-layouts: 5.48 us -> 9.97 us
    dot_general x17 -> x0, matrix products: 107 us -> none  [the longest x4 93.4 us: stop_update(): predicted = jnp.dot(user_bf, block.T, preferred_element_type=jnp.float32)]
    psum x1 -> x0, waiting for transfers between devices: 88.7 us -> none  [body(): grad_sum = lax.psum(grad_dense, ('blk', 'rep'))]
    pallas_call x0 -> x1, Pallas kernels: none -> 65.1 us  [body(): pl.pallas_call(functools.partial(kernel, n_blk, n_rep), out_shape=(jax.Sh...]
    ppermute x4 -> x0, waiting for transfers between devices: 37.3 us -> none  [from_behind(): return lax.ppermute(block, axis, route)]
    unnamed x44 -> x21, local copies, waits for them, and re-layouts: 2.94 us -> 9.97 us
    all_gather x1 -> x0, blocking collectives: 5.95 us -> none  [body(): lax.all_gather(hot_factors.astype(jnp.bfloat16), 'rep', axis=0, tiled=True)]
    convert_element_type x5 -> x0, other arithmetic: 3.39 us -> none  [the longest x4 2.42 us: build_block(): slot_values[position].astype(jnp.float32)[:, None]]
  transfers between devices with their start and end apart: 5 -> 0, of which waited for: 4 -> 0; matrix products, arithmetic and copies ran while one was open for 13% -> 0% of each run, Pallas kernels for 0% -> 0%
where the time goes in v1:
time: 76.8 us; the launch traced here: 76.4 us
  Pallas kernels  65.1 us (85%)
  local copies, waits for them, and re-layouts  9.97 us (13%)
  between operations  1.33 us (2%)
    pallas_call x1, Pallas kernels, body(): pl.pallas_call(functools.partial(kernel, n_blk, n_rep), out_shape=(jax.Sh...  65.1 us
    unnamed x21, local copies, waits for them, and re-layouts  9.97 us

profile of v1, /device:TPU:1, one launch (start us, length us, event | category | flops | bytes accessed | tf_op | source)
XLA Modules:
  0.0 76.4 jit_solution(18214562787225006776)
XLA Ops:
  0.6 0.0 copy-start.7
  1.3 0.0 copy-start.8
  1.3 0.0 copy-done.7
  1.3 0.7 copy-done.8
  2.0 0.0 copy-start
  2.0 1.2 %copy-done = f32[1024,256]{1,0:T(8,128)S(1)} copy-done((f32[1024,256]{1,0:T(8,128)S(1)}, f32[1024,256]{1,0:T(8,128)}, u32[]{:S(2)}) %copy-start) | copy-done | bytes 1048600
  3.2 0.0 copy-start.1
  3.2 1.0 %copy-done.1 = bf16[1024,256]{1,0:T(8,128)(2,1)S(1)} copy-done((bf16[1024,256]{1,0:T(8,128)(2,1)S(1)}, bf16[1024,256]{1,0:T(8,128)(2,1)}, u32[]{:S(2)}) %copy-start.1) | copy-done | bytes 524312
  4.2 0.0 copy-start.2
  4.3 1.0 %copy-done.2 = bf16[1024,256]{1,0:T(8,128)(2,1)S(1)} copy-done((bf16[1024,256]{1,0:T(8,128)(2,1)S(1)}, bf16[1024,256]{1,0:T(8,128)(2,1)}, u32[]{:S(2)}) %copy-start.2) | copy-done | bytes 524312
  5.3 0.0 copy-start.3
  5.3 0.9 %copy-done.3 = f32[256,256]{1,0:T(8,128)S(1)} copy-done((f32[256,256]{1,0:T(8,128)S(1)}, f32[256,256]{1,0:T(8,128)}, u32[]{:S(2)}) %copy-start.3) | copy-done | bytes 262168
  6.2 0.0 copy-start.4
  6.2 0.9 %copy-done.4 = s32[4,16,1024]{2,1,0:T(8,128)S(1)} copy-done((s32[4,16,1024]{2,1,0:T(8,128)S(1)}, s32[4,16,1024]{2,1,0:T(8,128)}, u32[]{:S(2)}) %copy-start.4) | copy-done | bytes 262168
  7.2 0.0 copy-start.5
  7.2 0.9 %copy-done.5 = bf16[4,16,1024]{2,1,0:T(8,128)(2,1)S(1)} copy-done((bf16[4,16,1024]{2,1,0:T(8,128)(2,1)S(1)}, bf16[4,16,1024]{2,1,0:T(8,128)(2,1)}, u32[]{:S(2)}) %copy-start.5) | copy-done | bytes 131096
  8.1 0.0 copy-start.6
  8.1 0.7 copy-done.6
  8.8 65.1 %shard_map.121 = (f32[1024,256]{1,0:T(8,128)S(1)}, bf16[1024,256]{1,0:T(8,128)(2,1)S(1)}, f32[256,256]{1,0:T(8,128)S(1)}) custom-call(f32[1024,256]{1,0:T(8,128)S(1)} %copy-done, bf16[1024,256]{1,0:T(8,128)(2,1)S(1)} %copy-done.1, f32[256,256]{1,0:T(8,128)S(1)} %copy-done.3, s32[4,16,1024]{2,1,0:T(8,128)S(1)} %copy-done.4, ...), custom_call_target="tpu_custom_call" | custom-call | tf_op jit(solution)/shard_map/pallas_call | solution.py:418
  73.9 1.0 %copy.17 = f32[1024,256]{1,0:T(8,128)} copy(f32[1024,256]{1,0:T(8,128)S(1)} %get-tuple-element.6) | data formatting | bytes 2097152
  74.9 0.8 %copy.18 = bf16[1024,256]{1,0:T(8,128)(2,1)} copy(bf16[1024,256]{1,0:T(8,128)(2,1)S(1)} %get-tuple-element.7) | data formatting | bytes 1048576
  75.7 0.7 copy.19
Async XLA Ops:
  0.6 0.7 copy-start.7
  1.3 0.7 copy-start.8
  2.0 1.2 %copy-start = (f32[1024,256]{1,0:T(8,128)S(1)}, f32[1024,256]{1,0:T(8,128)}, u32[]{:S(2)}) copy-start(f32[1024,256]{1,0:T(8,128)} %users_ref.1) | copy-start | bytes 3145732
  3.2 1.0 %copy-start.1 = (bf16[1024,256]{1,0:T(8,128)(2,1)S(1)}, bf16[1024,256]{1,0:T(8,128)(2,1)}, u32[]{:S(2)}) copy-start(bf16[1024,256]{1,0:T(8,128)(2,1)} %items_ref.1) | copy-start | bytes 1572868
  4.2 1.0 %copy-start.2 = (bf16[1024,256]{1,0:T(8,128)(2,1)S(1)}, bf16[1024,256]{1,0:T(8,128)(2,1)}, u32[]{:S(2)}) copy-start(bf16[1024,256]{1,0:T(8,128)(2,1)} %hot_values_ref.1) | copy-start | bytes 1572868
  5.3 0.9 %copy-start.3 = (f32[256,256]{1,0:T(8,128)S(1)}, f32[256,256]{1,0:T(8,128)}, u32[]{:S(2)}) copy-start(f32[256,256]{1,0:T(8,128)} %hot_ref.1) | copy-start | bytes 786436
  6.2 0.9 %copy-start.4 = (s32[4,16,1024]{2,1,0:T(8,128)S(1)}, s32[4,16,1024]{2,1,0:T(8,128)}, u32[]{:S(2)}) copy-start(s32[4,16,1024]{2,1,0:T(8,128)} %slot_items_ref.1) | copy-start | bytes 786436
  7.2 0.9 %copy-start.5 = (bf16[4,16,1024]{2,1,0:T(8,128)(2,1)S(1)}, bf16[4,16,1024]{2,1,0:T(8,128)(2,1)}, u32[]{:S(2)}) copy-start(bf16[4,16,1024]{2,1,0:T(8,128)(2,1)} %slot_values_ref.1) | copy-start | bytes 393220
  8.1 0.7 copy-start.6

commit v2 on v1

--- a/solution.py
+++ b/solution.py
@@ -49,16 +49,16 @@
 def kernel(
     n_blk,
     n_rep,
-    users_ref,
-    items_ref,
-    hot_ref,
-    slot_items_ref,
-    slot_values_ref,
-    slot_lengths_ref,
-    hot_ids_ref,
+    users_hbm,
+    items_hbm,
+    hot_hbm,
+    slot_items_hbm,
+    slot_values_hbm,
+    slot_lengths_hbm,
+    hot_ids_hbm,
     hot_count_ref,
-    hot_values_ref,
-    hot_lengths_ref,
+    hot_values_hbm,
+    hot_lengths_hbm,
     users_out,
     items_out,
     hot_out,
@@ -77,6 +77,18 @@
     grads,
     reps_in,
     hot_new,
+    users_ref,
+    items_ref,
+    hot_ref,
+    slot_items_ref,
+    slot_values_ref,
+    slot_lengths_ref,
+    hot_ids_ref,
+    hot_values_ref,
+    hot_lengths_ref,
+    hot_err_ref,
+    user_t_hot,
+    load_sem,
     *rest,
 ):
     users_n, rank = users_ref.shape
@@ -100,6 +112,23 @@
         back_recv,
     ) = rest[len(plan) :]
 
+    def load(k, source, target):
+        return pltpu.make_async_copy(source, target, load_sem.at[k])
+
+    loads = {
+        "hot": load(0, hot_hbm, hot_ref),
+        "slot_items": load(1, slot_items_hbm, slot_items_ref),
+        "slot_values": load(2, slot_values_hbm, slot_values_ref),
+        "slot_lengths": load(3, slot_lengths_hbm, slot_lengths_ref),
+        "users": load(4, users_hbm, users_ref),
+        "items": load(5, items_hbm, items_ref),
+        "hot_values": load(6, hot_values_hbm, hot_values_ref),
+        "hot_ids": load(7, hot_ids_hbm, hot_ids_ref),
+        "hot_lengths": load(8, hot_lengths_hbm, hot_lengths_ref),
+    }
+    for copy in loads.values():
+        copy.start()
+
     b, r = lax.axis_index("blk"), lax.axis_index("rep")
     wrap = r == n_rep - 1
     nxt = (jnp.where(wrap, lax.rem(b + 1, n_blk), b), lax.rem(r + 1, n_rep))
@@ -122,6 +151,7 @@
     pl.semaphore_wait(barrier, len(peers))
 
     own_at = pl.ds(pl.multiple_of(r * own_hot, own_hot), own_hot)
+    loads["hot"].wait()
     hot_full[own_at, :] = hot_ref[...].astype(BF16)
     gathers = []
     for k in range(1, n_rep):
@@ -137,13 +167,6 @@
         gathers.append(copy)
 
     eye[...] = one_hot(iota(eye.shape, 0) == iota(eye.shape, 1)).astype(BF16)
-
-    def to_blocks(c, carry):
-        rows = items_ref[pl.ds(pl.multiple_of(c * CHUNK, CHUNK), CHUNK), :]
-        blocks[0, c] = nt(eye[...], rows).astype(BF16)
-        return carry
-
-    lax.fori_loop(0, n_chunks, to_blocks, 0)
 
     lines = 3 * slots
     cols = slots * GROUP
@@ -189,14 +212,26 @@
 
         lax.fori_loop(0, n_groups // 8, eight, 0)
 
-    def transpose_users():
+    def transpose_users(target):
         for i in range(users_n // CHUNK):
             rows = slice(i * CHUNK, (i + 1) * CHUNK)
-            user_t[:, rows] = nt(eye[...], user_bf[rows, :]).astype(BF16)
-
+            target[:, rows] = nt(eye[...], user_bf[rows, :]).astype(BF16)
+
+    for name in ("slot_items", "slot_values", "slot_lengths"):
+        loads[name].wait()
+    expand(0)
+    for name in ("users", "items", "hot_values", "hot_ids", "hot_lengths"):
+        loads[name].wait()
     user_bf[...] = users_ref[...].astype(BF16)
-    transpose_users()
-    expand(0)
+    transpose_users(user_t_hot)
+
+    def to_blocks(c, carry):
+        rows = items_ref[pl.ds(pl.multiple_of(c * CHUNK, CHUNK), CHUNK), :]
+        blocks[0, c] = nt(eye[...], rows).astype(BF16)
+        return carry
+
+    lax.fori_loop(0, n_chunks, to_blocks, 0)
+
 
     for copy in gathers:
         copy.wait()
@@ -218,18 +253,20 @@
         bound = nt(eye[...], jnp.broadcast_to(limit[:, rows], (hot_slots, CHUNK)))
         valid = iota(predicted.shape, 1).astype(F32) < bound
         hot_err = jnp.where(valid, hot_values_ref[rows, :].astype(F32) - predicted, 0.0).astype(BF16)
-        err[rows, :] = hot_err
+        hot_err_ref[rows, :] = hot_err
         pulled = nt(hot_err, hot_slot_t)
         old = users_ref[rows, :]
         users_out[rows, :] = old + user_rate * (pulled - DECAY_RATE * old)
-    slot_grads = nn(user_t[...], err[...])
-    dense = jnp.zeros((hot_total, rank), F32)
-    for _ in range(3):
-        piece = slot_grads.astype(BF16)
-        dense = dense + nt(selector, piece)
-        slot_grads = slot_grads - piece.astype(F32)
-    for i in range(n_rep):
-        grads[i] = dense[i * own_hot : (i + 1) * own_hot, :]
+
+    def hot_grads():
+        slot_grads = nn(user_t_hot[...], hot_err_ref[...])
+        dense = jnp.zeros((hot_total, rank), F32)
+        for _ in range(3):
+            piece = slot_grads.astype(BF16)
+            dense = dense + nt(selector, piece)
+            slot_grads = slot_grads - piece.astype(F32)
+        for i in range(n_rep):
+            grads[i] = dense[i * own_hot : (i + 1) * own_hot, :]
 
     def reduce_steps():
         low = 0
@@ -324,13 +361,15 @@
 
     for t in range(stops):
         user_bf[...] = users_out[...].astype(BF16)
-        transpose_users()
+        transpose_users(user_t)
         grad_users[...] = jnp.zeros_like(grad_users)
         if t > 0:
             expand(t)
             next(steps, None)
         half = n_chunks // 2
         lax.fori_loop(0, half, functools.partial(chunk, t), 0)
+        if t == 0:
+            hot_grads()
         next(steps, None)
         lax.fori_loop(half, n_chunks, functools.partial(chunk, t), 0)
         next(steps, None)
@@ -379,7 +418,7 @@
     plan, held_rows = reduce_plan(n_blk, own_hot)
     dma = pltpu.SemaphoreType.DMA
     vmem = pl.BlockSpec(memory_space=pltpu.VMEM)
-    specs = [vmem] * 10
+    specs = [pl.BlockSpec(memory_space=pltpu.HBM)] * 10
     specs[7] = pl.BlockSpec(memory_space=pltpu.SMEM)
     scratch = [
         pltpu.VMEM((CHUNK, CHUNK), BF16),
@@ -397,6 +436,18 @@
         pltpu.VMEM((n_rep, own_hot, rank), F32),
         pltpu.VMEM((max(n_rep - 1, 1), held_rows, rank), F32),
         pltpu.VMEM((own_hot, rank), F32),
+        pltpu.VMEM(users.shape, F32),
+        pltpu.VMEM(items.shape, BF16),
+        pltpu.VMEM(hot_factors.shape, F32),
+        pltpu.VMEM(slot_items.shape, jnp.int32),
+        pltpu.VMEM(slot_values.shape, BF16),
+        pltpu.VMEM(slot_lengths.shape, jnp.int32),
+        pltpu.VMEM((1, hot_ids.shape[0]), jnp.int32),
+        pltpu.VMEM(hot_values.shape, BF16),
+        pltpu.VMEM((1, users_n), jnp.int32),
+        pltpu.VMEM(hot_values.shape, BF16),
+        pltpu.VMEM((rank, users_n), BF16),
+        dma((9,)),
     ]
     for _, held, halve in plan:
         scratch.append(pltpu.VMEM((n_rep, held // 2 if halve else held, rank), F32))
@@ -426,7 +477,7 @@
             out_specs=(vmem, vmem, vmem),
             scratch_shapes=scratch,
             compiler_params=pltpu.CompilerParams(
-                collective_id=0, has_side_effects=True, vmem_limit_bytes=48 * 2**20
+                collective_id=0, has_side_effects=True, vmem_limit_bytes=63 * 2**20
             ),
         )(
             users,

time: 76.8 us -> 71.6 us (0.932)
  local copies, waits for them, and re-layouts: 9.97 us -> 4.12 us
  Pallas kernels: 65.1 us -> 66 us
    unnamed x21 -> x7, local copies, waits for them, and re-layouts: 9.97 us -> 4.12 us
    pallas_call x1, Pallas kernels: 65.1 us -> 66 us  [body(): pl.pallas_call(functools.partial(kernel, n_blk, n_rep), out_shape=(jax.Sh...]
where the time goes in v2:
time: 71.6 us; the launch traced here: 71.4 us
  Pallas kernels  66 us (92%)
  local copies, waits for them, and re-layouts  4.12 us (6%)
  between operations  1.3 us (2%)
    pallas_call x1, Pallas kernels, body(): pl.pallas_call(functools.partial(kernel, n_blk, n_rep), out_shape=(jax.Sh...  66 us
    unnamed x7, local copies, waits for them, and re-layouts  4.12 us

profile of v2, /device:TPU:1, one launch (start us, length us, event | category | flops | bytes accessed | tf_op | source)
XLA Modules:
  0.0 71.4 jit_solution(9088067799638143283)
XLA Ops:
  1.3 66.0 %shard_map.121 = (f32[1024,256]{1,0:T(8,128)}, bf16[1024,256]{1,0:T(8,128)(2,1)}, f32[256,256]{1,0:T(8,128)}) custom-call(f32[1024,256]{1,0:T(8,128)} %users_hbm.1, bf16[1024,256]{1,0:T(8,128)(2,1)} %items_hbm.1, f32[256,256]{1,0:T(8,128)} %hot_hbm.1, s32[4,16,1024]{2,1,0:T(8,128)} %slot_items_hbm.1, bf16[4,16,1024]{2,1,0:T(8,128)(2,1)} %slot_values_hbm.1, ...), custom_call_target="tpu_custom_call" | custom-call | tf_op jit(solution)/shard_map/pallas_call | solution.py:469
  67.3 0.0 copy-start
  67.3 2.3 %copy.17 = f32[1024,256]{1,0:T(8,128)} copy(f32[1024,256]{1,0:T(8,128)} %get-tuple-element.6) | data formatting | bytes 2097152
  69.6 0.0 copy-done
  69.6 0.0 copy-start.1
  69.7 0.8 %copy.18 = bf16[1024,256]{1,0:T(8,128)(2,1)} copy(bf16[1024,256]{1,0:T(8,128)(2,1)S(1)} %copy-done) | data formatting | bytes 1048576
  70.4 0.3 copy-done.1
  70.7 0.7 copy.19
Async XLA Ops:
  67.3 2.3 %copy-start = (bf16[1024,256]{1,0:T(8,128)(2,1)S(1)}, bf16[1024,256]{1,0:T(8,128)(2,1)}, u32[]{:S(2)}) copy-start(bf16[1024,256]{1,0:T(8,128)(2,1)} %get-tuple-element.7) | copy-start | bytes 1572868
  69.6 1.1 %copy-start.1 = (f32[256,256]{1,0:T(8,128)S(1)}, f32[256,256]{1,0:T(8,128)}, u32[]{:S(2)}) copy-start(f32[256,256]{1,0:T(8,128)} %get-tuple-element.8) | copy-start | bytes 786436

commit v3 on v2

--- a/solution.py
+++ b/solution.py
@@ -372,7 +372,8 @@
             hot_grads()
         next(steps, None)
         lax.fori_loop(half, n_chunks, functools.partial(chunk, t), 0)
-        next(steps, None)
+        if t == 0:
+            next(steps, None)
         old = users_out[...]
         users_out[...] = old + LEARN_RATE * (grad_users[...] - DECAY_RATE * old)
 
@@ -394,6 +395,15 @@
             return carry
 
         lax.fori_loop(0, n_chunks, drain, 0)
+
+
+def write_out(*refs):
+    *refs, sem = refs
+    copies = [pltpu.make_async_copy(refs[i], refs[i + 3], sem.at[i]) for i in range(3)]
+    for copy in copies:
+        copy.start()
+    for copy in copies:
+        copy.wait()
 
 
 def body(
@@ -465,7 +475,7 @@
         dma((bits,)),
         dma((bits,)),
     ]
-    return tuple(
+    outs = tuple(
         pl.pallas_call(
             functools.partial(kernel, n_blk, n_rep),
             out_shape=(
@@ -492,6 +502,16 @@
             hot_lengths.reshape(1, -1),
         )
     )
+    hbm = pl.BlockSpec(memory_space=pltpu.HBM)
+    return tuple(
+        pl.pallas_call(
+            write_out,
+            out_shape=tuple(jax.ShapeDtypeStruct(x.shape, x.dtype) for x in outs),
+            in_specs=[hbm] * 3,
+            out_specs=(hbm,) * 3,
+            scratch_shapes=[dma((3,))],
+        )(*outs)
+    )
 
 
 def solution(mesh):

time: 71.6 us -> 124 us (1.73); the launches traced: 71.4 us -> 122 us
  Pallas kernels: 66 us -> 121 us
  local copies, waits for them, and re-layouts: 4.12 us -> 0 us
    pallas_call x0 -> x1, Pallas kernels: none -> 56.7 us  [body(): pl.pallas_call(write_out, out_shape=tuple((jax.ShapeDtypeStruct(x.shape,...]
    unnamed x7 -> x0, local copies, waits for them, and re-layouts: 4.12 us -> none
    pallas_call x1, Pallas kernels: 66 us -> 64.1 us  [body(): pl.pallas_call(functools.partial(kernel, n_blk, n_rep), out_shape=(jax.Sh...]
where the time goes in v3:
time: 124 us; the launch traced here: 122 us
  Pallas kernels  121 us (98%)
  between operations  1.29 us (1%)
    pallas_call x1, Pallas kernels, body(): pl.pallas_call(functools.partial(kernel, n_blk, n_rep), out_shape=(jax.Sh...  64.1 us
    pallas_call x1, Pallas kernels, body(): pl.pallas_call(write_out, out_shape=tuple((jax.ShapeDtypeStruct(x.shape,...  56.7 us

profile of v3, /device:TPU:1, one launch (start us, length us, event | category | flops | bytes accessed | tf_op | source)
XLA Modules:
  0.0 122.1 jit_solution(15440322889485760748)
XLA Ops:
  1.3 64.1 %shard_map.121 = (f32[1024,256]{1,0:T(8,128)}, bf16[1024,256]{1,0:T(8,128)(2,1)}, f32[256,256]{1,0:T(8,128)}) custom-call(f32[1024,256]{1,0:T(8,128)} %users_hbm.1, bf16[1024,256]{1,0:T(8,128)(2,1)} %items_hbm.1, f32[256,256]{1,0:T(8,128)} %hot_hbm.1, s32[4,16,1024]{2,1,0:T(8,128)} %slot_items_hbm.1, bf16[4,16,1024]{2,1,0:T(8,128)(2,1)} %slot_values_hbm.1, ...), custom_call_target="tpu_custom_call" | custom-call | tf_op jit(solution)/shard_map/pallas_call | solution.py:479
  65.4 56.7 %shard_map.122 = (f32[1024,256]{1,0:T(8,128)}, bf16[1024,256]{1,0:T(8,128)(2,1)}, f32[256,256]{1,0:T(8,128)}) custom-call(f32[1024,256]{1,0:T(8,128)} %get-tuple-element.6.refs_0_, bf16[1024,256]{1,0:T(8,128)(2,1)} %get-tuple-element.7.refs_1_, f32[256,256]{1,0:T(8,128)} %get-tuple-element.8.refs_2_), custom_call_target="tpu_custom_call" | custom-call | tf_op jit(solution)/shard_map/pallas_call | solution.py:507
